TPU v7x, 512 devices: a whole 4x8x8 slice. The times are simulated.
512 devices in a mesh: seg: 128 (over z, x, y_hi, core), head: 4 (over y_lo).
Axes of the slice: x: 4, y: 8 (y_hi: 2, y_lo: 4; y = y_hi * 4 + y_lo), z: 8, core: 2. Of those that a mesh axis runs over, the one named last changes fastest.
Arguments:
- layer_input: bfloat16 [1, 65536, 2048], P(None, 'seg', 'head'), may hold values from -160 to 160, as said below
- w_qkv: bfloat16 [2048, 3, 1024], P(None, None, 'head'), may hold values from -3 to 3
- comp_weight: bfloat16 [3, 2, 1024], P(None, None, 'head'), may hold values from -2.5 to 2.5
- w_out: bfloat16 [1024, 2048], P('seg', 'head'), may hold values from -1.5 to 1.5
Outputs:
- attn_out: bfloat16 [1, 65536, 2048], P(None, 'seg', 'head')
Inputs may be any that keep to these rules, and one draw needn't show every extreme that they name: layer_input varies in scale from feature to feature and from token to token.
All inputs are finite; a program needn't handle non-finite values.
Results may differ from a plain program's by a relative error of at most 0.0089.
Values may be sent and summed in bfloat16 or wider, within the bound.
A program may use at most 64 MiB of HBM per device.

v0:
```python
import math

import jax
import jax.numpy as jnp
from jax import lax
from jax.sharding import PartitionSpec as P

DH = 128


def sent_to_all(x, axis):
    copies = jnp.broadcast_to(x, (lax.axis_size(axis), *x.shape))
    return lax.all_to_all(copies, axis, split_axis=0, concat_axis=0, tiled=True)


def laid_out(tiles, dim):
    shape = list(tiles.shape[1:])
    shape[dim] *= tiles.shape[0]
    return jnp.moveaxis(tiles, 0, dim).reshape(shape)


def collect(x, axis, dim):
    tiles = sent_to_all(x, axis)
    return laid_out(tiles, dim)


def passed_along(block, axis, distance):
    devices = range(lax.axis_size(axis))
    route = [(i - distance, i) for i in devices if i - distance in devices]
    return lax.ppermute(block, axis, route)


def layer_norm(values):
    center_mean = jnp.mean(values, axis=-1, keepdims=True)
    centered = values - center_mean
    variance = jnp.mean(centered * centered, axis=-1, keepdims=True)
    return centered * lax.rsqrt(variance + 1e-05)


def compress_block(source, weight):
    batch, pair, length, width = source.shape
    grouped = source.reshape(batch, pair, length // 3, 3, width)
    mixed = jnp.einsum("bkltc,tkc->bklc", grouped, weight, preferred_element_type=jnp.float32)
    return mixed.astype(jnp.bfloat16)


def key_allowed(seg_len, segment):
    query_pos = jnp.arange(seg_len)[:, None]
    key_pos = jnp.arange(3 * seg_len)[None, :]
    own_part = (key_pos >= 2 * seg_len) & (key_pos - 2 * seg_len <= query_pos)
    memory_part = (key_pos >= seg_len) & (key_pos < 2 * seg_len) & (segment >= 1)
    comp_part = (key_pos < seg_len) & (segment >= 4)
    return own_part | memory_part | comp_part


def attend(queries, key_vals, segment):
    batch, seg_len, width = queries.shape
    heads_here = width // DH
    query_heads = queries.reshape(batch, seg_len, heads_here, DH)
    key_heads = key_vals[:, 0].reshape(batch, 3 * seg_len, heads_here, DH)
    value_heads = key_vals[:, 1].reshape(batch, 3 * seg_len, heads_here, DH)
    scores = jnp.einsum(
        "bqhd,bkhd->bhqk", query_heads, key_heads, preferred_element_type=jnp.float32
    )
    scores = scores / math.sqrt(DH)
    allowed = key_allowed(seg_len, segment)
    scores = jnp.where(allowed[None, None], scores, jnp.float32(-1e30))
    highest = jnp.max(scores, axis=-1, keepdims=True)
    exponent = jnp.exp(scores - highest)
    weights = (exponent / jnp.sum(exponent, axis=-1, keepdims=True)).astype(jnp.bfloat16)
    mixed = jnp.einsum("bhqk,bkhd->bqhd", weights, value_heads, preferred_element_type=jnp.float32)
    return mixed.astype(jnp.bfloat16).reshape(batch, seg_len, width)


def local(layer_input, w_qkv, comp_weight, w_out):
    gathered = collect(layer_input, "head", 2)
    normed = layer_norm(gathered.astype(jnp.float32)).astype(jnp.bfloat16)
    projected = jnp.einsum("bld,dkc->bklc", normed, w_qkv, preferred_element_type=jnp.float32)
    projected = projected.astype(jnp.bfloat16)
    queries = projected[:, 0]
    key_vals = projected[:, 1:3]
    memory = passed_along(key_vals, "seg", 1)
    earlier_kv = [passed_along(key_vals, "seg", distance) for distance in (4, 3, 2)]
    compressed = compress_block(jnp.concatenate(earlier_kv, axis=2), comp_weight)
    segment = lax.axis_index("seg")
    joined = jnp.concatenate([compressed, memory, key_vals], axis=2)
    context = attend(queries, joined, segment)
    full_ctx = collect(context, "head", 2)
    whole_out = lax.all_gather(w_out, "seg", axis=0, tiled=True)
    result_sum = jnp.einsum("blr,rc->blc", full_ctx, whole_out, preferred_element_type=jnp.float32)
    return result_sum.astype(jnp.bfloat16)


def solution(mesh):
    return jax.shard_map(
        local,
        mesh=mesh,
        in_specs=(
            P(None, "seg", "head"),
            P(None, None, "head"),
            P(None, None, "head"),
            P("seg", "head"),
        ),
        out_specs=P(None, "seg", "head"),
        check_vma=False,
    )
```

profile of v0, /device:TPU:448, one launch (start us, length us, event | category | flops | bytes accessed | tf_op | source)
XLA Modules:
  0.0 188.4 jit_solution(15708641360451684064)
XLA Ops:
  6.5 2.7 %broadcast_in_dim.16 = bf16[4,1,512,512]{3,2,1,0:T(8,128)(2,1)} broadcast(bf16[512,512]{1,0:T(8,128)(2,1)} %bitcast.68), dimensions={2,3} | broadcast | bytes 2621440 | tf_op jit(solution)/shard_map/broadcast_in_dim | solution.py:12
  9.2 4.9 %all-to-all-start = ((bf16[4,1,512,512]{3,2,1,0:T(8,128)(2,1)}), bf16[4,1,512,512]{3,2,1,0:T(8,128)(2,1)}, u32[]{:S(2)}, u32[]{:S(2)}) async-start(bf16[4,1,512,512]{3,2,1,0:T(8,128)(2,1)} %broadcast_in_dim.16), calls=%async_computation | async-start | bytes 4194304 | tf_op jit(solution)/shard_map/all_to_all | solution.py:13
  14.1 0.7 all-gather.2.cloned.1.call-update
  14.8 47.7 %all-to-all-done = bf16[4,1,512,512]{3,2,1,0:T(8,128)(2,1)} async-done(((bf16[4,1,512,512]{3,2,1,0:T(8,128)(2,1)}), bf16[4,1,512,512]{3,2,1,0:T(8,128)(2,1)}, u32[]{:S(2)}, u32[]{:S(2)}) %all-to-all-start) | async-done | bytes 2097184 | tf_op jit(solution)/shard_map/all_to_all | solution.py:13
  62.5 4.2 %copy.18 = bf16[4,1,512,512]{2,3,0,1:T(8,128)(2,1)} copy(bf16[4,1,512,512]{3,2,1,0:T(8,128)(2,1)} %all-to-all-done) | data formatting | bytes 4194304 | tf_op jit(solution)/shard_map/all_to_all | solution.py:13
  66.7 2.1 %convert_reduce_fusion = f32[512]{0:T(512)S(1)} fusion(bf16[4,1,512,512]{2,3,0,1:T(8,128)(2,1)} %copy.18), kind=kLoop, calls=%fused_computation.29 | loop fusion | flops 2096640 | bytes 2099200 | tf_op jit(solution)/shard_map/reduce_sum | solution.py:34
  68.8 0.1 copy-done.1
  68.9 0.6 fusion.3
  69.5 0.5 fusion.5
  70.0 1.8 fusion.18
  71.9 0.8 slice.16
  72.7 3.4 %collective-permute-start = (bf16[1,2,512,256]{2,3,1,0:T(8,128)(2,1)}, bf16[1,2,512,256]{2,3,1,0:T(8,128)(2,1)S(1)}, u32[]{:S(2)}, u32[]{:S(2)}) collective-permute-start(bf16[1,2,512,256]{2,3,1,0:T(8,128)(2,1)} %slice.16), channel_id=1, source_target_pairs={{0,16},{4,20},{8,24},{12,28},{16,32},{20,36},{24,40},{28,44},{32,4... | collective-permute-start | bytes 1572872 | tf_op jit(solution)/shard_map/ppermute | solution.py:30
  76.1 6.0 %collective-permute-start.1 = (bf16[1,2,512,256]{2,3,1,0:T(8,128)(2,1)}, bf16[1,2,512,256]{2,3,1,0:T(8,128)(2,1)S(1)}, u32[]{:S(2)}, u32[]{:S(2)}) collective-permute-start(bf16[1,2,512,256]{2,3,1,0:T(8,128)(2,1)} %slice.16), channel_id=1, source_target_pairs={{0,12},{4,16},{8,20},{12,24},{16,28},{20,32},{24,36},{28,40},{32,4... | collective-permute-start | bytes 1572872 | tf_op jit(solution)/shard_map/ppermute | solution.py:30
  82.1 3.5 %collective-permute-start.2 = (bf16[1,2,512,256]{2,3,1,0:T(8,128)(2,1)}, bf16[1,2,512,256]{2,3,1,0:T(8,128)(2,1)S(1)}, u32[]{:S(2)}, u32[]{:S(2)}) collective-permute-start(bf16[1,2,512,256]{2,3,1,0:T(8,128)(2,1)} %slice.16), channel_id=1, source_target_pairs={{0,8},{4,12},{8,16},{12,20},{16,24},{20,28},{24,32},{28,36},{32,40... | collective-permute-start | bytes 1572872 | tf_op jit(solution)/shard_map/ppermute | solution.py:30
  85.6 1.6 fusion.10
  87.2 3.4 %collective-permute-start.3 = (bf16[1,2,512,256]{2,3,1,0:T(8,128)(2,1)}, bf16[1,2,512,256]{2,3,1,0:T(8,128)(2,1)}, u32[]{:S(2)}, u32[]{:S(2)}) collective-permute-start(bf16[1,2,512,256]{2,3,1,0:T(8,128)(2,1)} %slice.16), channel_id=1, source_target_pairs={{0,4},{4,8},{8,12},{12,16},{16,20},{20,24},{24,28},{28,32},{32,36}... | collective-permute-start | bytes 1572872 | tf_op jit(solution)/shard_map/ppermute | solution.py:30
  90.7 3.7 %collective-permute-done = bf16[1,2,512,256]{2,3,1,0:T(8,128)(2,1)S(1)} collective-permute-done((bf16[1,2,512,256]{2,3,1,0:T(8,128)(2,1)}, bf16[1,2,512,256]{2,3,1,0:T(8,128)(2,1)S(1)}, u32[]{:S(2)}, u32[]{:S(2)}) %collective-permute-start) | collective-permute-done | bytes 524320 | tf_op jit(solution)/shard_map/ppermute | solution.py:30
  94.4 20.1 %collective-permute-done.1 = bf16[1,2,512,256]{2,3,1,0:T(8,128)(2,1)S(1)} collective-permute-done((bf16[1,2,512,256]{2,3,1,0:T(8,128)(2,1)}, bf16[1,2,512,256]{2,3,1,0:T(8,128)(2,1)S(1)}, u32[]{:S(2)}, u32[]{:S(2)}) %collective-permute-start.1) | collective-permute-done | bytes 524320 | tf_op jit(solution)/shard_map/ppermute | solution.py:30
  114.5 17.1 %collective-permute-done.2 = bf16[1,2,512,256]{2,3,1,0:T(8,128)(2,1)S(1)} collective-permute-done((bf16[1,2,512,256]{2,3,1,0:T(8,128)(2,1)}, bf16[1,2,512,256]{2,3,1,0:T(8,128)(2,1)S(1)}, u32[]{:S(2)}, u32[]{:S(2)}) %collective-permute-start.2) | collective-permute-done | bytes 524320 | tf_op jit(solution)/shard_map/ppermute | solution.py:30
  131.6 1.2 pad_maximum_fusion
  132.9 4.9 %copy.38 = bf16[1,2,1536,256]{3,1,2,0:T(2,128)(2,1)} copy(bf16[1,2,1536,256]{2,3,1,0:T(8,128)(2,1)} %pad_maximum_fusion) | data formatting | bytes 3145728
  137.8 5.0 %multiply_reduce_fusion = bf16[2,256,512]{1,0,2:T(2,128)(2,1)} fusion(bf16[2,256,3,512]{1,0,2,3:T(2,128)(2,1)} %bitcast.63, f32[2,256,3]{1,0,2:T(2,128)S(1)} %bitcast_convert_fusion), kind=kLoop, calls=%fused_computation.11 | loop fusion | flops 2097152 | bytes 2103296
  142.8 2.0 %copy.34 = bf16[2,256,512]{2,1,0:T(8,128)(2,1)} copy(bf16[2,256,512]{1,0,2:T(2,128)(2,1)} %multiply_reduce_fusion) | data formatting | bytes 1048576 | tf_op jit(solution)/shard_map/bkltc,tkc->bklc/dot_general | solution.py:43
  144.8 1.5 pad_maximum_fusion.1
  146.3 1.3 fusion.35
  147.6 3.8 %fusion.36 = f32[2,512]{1,0:T(2,128)S(1)} fusion(pred[512,1536]{1,0:T(8,128)(4,1)} %fusion.10, bf16[512,2,128]{0,2,1:T(8,128)(2,1)S(1)} %bitcast.70, bf16[1536,2,128]{0,2,1:T(8,128)(2,1)} %bitcast.65), kind=kOutput, calls=%fused_computation.49 | convolution fusion | flops 408946176 | bytes 1839104 | tf_op jit(solution)/shard_map/sub | solution.py:69
  151.4 4.6 %fusion.22 = bf16[2,128,512]{2,1,0:T(8,128)(2,1)S(1)} fusion(bf16[1536,2,128]{0,2,1:T(8,128)(2,1)} %bitcast.67, f32[2,512]{1,0:T(2,128)S(1)} %fusion.36, pred[512,1536]{1,0:T(8,128)(4,1)} %fusion.10, bf16[512,2,128]{0,2,1:T(8,128)(2,1)} %bitcast.71, bf16[1536,2,128]{0,2,1:T(8,128)(2,1)} %bitcast.66), kind=kOutput, calls=%fused_computation.28 | convolution fusion | flops 813304320 | bytes 2887680 | tf_op jit(solution)/shard_map/bhqk,bkhd->bqhd/dot_general | solution.py:71
  156.0 1.1 broadcast_in_dim.28
  157.1 4.2 %all-to-all-start.1 = ((bf16[4,1,512,256]{2,3,1,0:T(8,128)(2,1)}), bf16[4,1,512,256]{2,3,1,0:T(8,128)(2,1)}, u32[]{:S(2)}, u32[]{:S(2)}) async-start(bf16[4,1,512,256]{2,3,1,0:T(8,128)(2,1)} %broadcast_in_dim.28), calls=%async_computation.1 | async-start | bytes 2097152 | tf_op jit(solution)/shard_map/all_to_all | solution.py:13
  161.4 0.0 all-gather.2.cloned.1.call-done
  161.4 17.1 %all-to-all-done.1 = bf16[4,1,512,256]{2,3,1,0:T(8,128)(2,1)} async-done(((bf16[4,1,512,256]{2,3,1,0:T(8,128)(2,1)}), bf16[4,1,512,256]{2,3,1,0:T(8,128)(2,1)}, u32[]{:S(2)}, u32[]{:S(2)}) %all-to-all-start.1) | async-done | bytes 1048608 | tf_op jit(solution)/shard_map/all_to_all | solution.py:13
  178.5 3.1 %fusion.21 = bf16[1,512,512]{2,1,0:T(8,128)(2,1)} fusion(bf16[512,1024]{0,1:T(8,128)(2,1)} %bitcast.25, bf16[1024,512]{1,0:T(8,128)(2,1)} %all-gather.2.cloned.1.call-done), kind=kOutput, calls=%fused_computation.27 | convolution fusion | flops 537133056 | bytes 2621440 | tf_op jit(solution)/shard_map/blr,rc->blc/dot_general | solution.py:90
  (16 shorter events, 0.1 us)
Async XLA Ops:
  6.5 63.5 %copy-start = (bf16[2048,3,256]{2,0,1:T(8,128)(2,1)S(1)}, bf16[2048,3,256]{2,0,1:T(8,128)(2,1)}, u32[]{:S(2)}) copy-start(bf16[2048,3,256]{2,0,1:T(8,128)(2,1)} %param.5) | copy-start | bytes 9437188
  6.5 8.3 %copy-start.3 = (bf16[3,2,256]{2,1,0:T(2,128)(2,1)S(1)}, bf16[3,2,256]{2,1,0:T(2,128)(2,1)}, u32[]{:S(2)}) copy-start(bf16[3,2,256]{2,1,0:T(2,128)(2,1)} %param.6) | copy-start | bytes 9220
  9.2 53.3 %all-to-all-start = ((bf16[4,1,512,512]{3,2,1,0:T(8,128)(2,1)}), bf16[4,1,512,512]{3,2,1,0:T(8,128)(2,1)}, u32[]{:S(2)}, u32[]{:S(2)}) async-start(bf16[4,1,512,512]{3,2,1,0:T(8,128)(2,1)} %broadcast_in_dim.16), calls=%async_computation | async-start | bytes 4194304 | tf_op jit(solution)/shard_map/all_to_all | solution.py:13
  14.1 147.3 %all-gather.2.cloned.1.call-start = ((), (), s32[]{:S(2)}) async-start(), calls=%async_computation.2 | async-start | bytes 1056768 | tf_op jit(solution)/shard_map/all_gather | solution.py:89
  66.7 2.2 %copy-start.1 = (bf16[4,1,512,512]{2,3,0,1:T(8,128)(2,1)S(1)}, bf16[4,1,512,512]{2,3,0,1:T(8,128)(2,1)}, u32[]{:S(2)}) copy-start(bf16[4,1,512,512]{2,3,0,1:T(8,128)(2,1)} %copy.18) | copy-start | bytes 6291460
  72.7 21.7 %collective-permute-start = (bf16[1,2,512,256]{2,3,1,0:T(8,128)(2,1)}, bf16[1,2,512,256]{2,3,1,0:T(8,128)(2,1)S(1)}, u32[]{:S(2)}, u32[]{:S(2)}) collective-permute-start(bf16[1,2,512,256]{2,3,1,0:T(8,128)(2,1)} %slice.16), channel_id=1, source_target_pairs={{0,16},{4,20},{8,24},{12,28},{16,32},{20,36},{24,40},{28,44},{32,4... | collective-permute-start | bytes 1572872 | tf_op jit(solution)/shard_map/ppermute | solution.py:30
  76.1 38.4 %collective-permute-start.1 = (bf16[1,2,512,256]{2,3,1,0:T(8,128)(2,1)}, bf16[1,2,512,256]{2,3,1,0:T(8,128)(2,1)S(1)}, u32[]{:S(2)}, u32[]{:S(2)}) collective-permute-start(bf16[1,2,512,256]{2,3,1,0:T(8,128)(2,1)} %slice.16), channel_id=1, source_target_pairs={{0,12},{4,16},{8,20},{12,24},{16,28},{20,32},{24,36},{28,40},{32,4... | collective-permute-start | bytes 1572872 | tf_op jit(solution)/shard_map/ppermute | solution.py:30
  82.1 49.5 %collective-permute-start.2 = (bf16[1,2,512,256]{2,3,1,0:T(8,128)(2,1)}, bf16[1,2,512,256]{2,3,1,0:T(8,128)(2,1)S(1)}, u32[]{:S(2)}, u32[]{:S(2)}) collective-permute-start(bf16[1,2,512,256]{2,3,1,0:T(8,128)(2,1)} %slice.16), channel_id=1, source_target_pairs={{0,8},{4,12},{8,16},{12,20},{16,24},{20,28},{24,32},{28,36},{32,40... | collective-permute-start | bytes 1572872 | tf_op jit(solution)/shard_map/ppermute | solution.py:30
  87.2 57.6 %collective-permute-start.3 = (bf16[1,2,512,256]{2,3,1,0:T(8,128)(2,1)}, bf16[1,2,512,256]{2,3,1,0:T(8,128)(2,1)}, u32[]{:S(2)}, u32[]{:S(2)}) collective-permute-start(bf16[1,2,512,256]{2,3,1,0:T(8,128)(2,1)} %slice.16), channel_id=1, source_target_pairs={{0,4},{4,8},{8,12},{12,16},{16,20},{20,24},{24,28},{28,32},{32,36}... | collective-permute-start | bytes 1572872 | tf_op jit(solution)/shard_map/ppermute | solution.py:30
  90.7 56.9 %copy-start.2 = (bf16[1,1,512,256]{2,3,1,0:T(8,128)(2,1)}, bf16[1,1,512,256]{2,3,1,0:T(8,128)(2,1)S(1)}, u32[]{:S(2)}) copy-start(bf16[1,1,512,256]{2,3,1,0:T(8,128)(2,1)S(1)} %slice.18) | copy-start | bytes 786436
  157.1 21.3 %all-to-all-start.1 = ((bf16[4,1,512,256]{2,3,1,0:T(8,128)(2,1)}), bf16[4,1,512,256]{2,3,1,0:T(8,128)(2,1)}, u32[]{:S(2)}, u32[]{:S(2)}) async-start(bf16[4,1,512,256]{2,3,1,0:T(8,128)(2,1)} %broadcast_in_dim.28), calls=%async_computation.1 | async-start | bytes 2097152 | tf_op jit(solution)/shard_map/all_to_all | solution.py:13
Sparse Core Ops, SparseCore 0:
  19.5 133.4 all-gather.1
where the time goes:
time: 190 us; the launch traced here: 188 us
  waiting for transfers between devices  106 us (56%)
  starting transfers between devices  25.3 us (13%)
  local copies, waits for them, and re-layouts  17.1 us (9%)
  between operations  13.5 us (7%)
  matrix products  13.3 us (7%)
  other arithmetic  12.7 us (7%)
    all_to_all x2, waiting for transfers between devices, sent_to_all(): return lax.all_to_all(copies, axis, split_axis=0, concat_axis=0, tiled=True)  64.7 us
    ppermute x4, waiting for transfers between devices, passed_along(): return lax.ppermute(block, axis, route)  40.9 us
    ppermute x4, starting transfers between devices, passed_along(): return lax.ppermute(block, axis, route)  16.2 us
    all_to_all x2, starting transfers between devices, sent_to_all(): return lax.all_to_all(copies, axis, split_axis=0, concat_axis=0, tiled=True)  9.1 us
    unnamed x2, other arithmetic  5.05 us
    unnamed x9, local copies, waits for them, and re-layouts  5.04 us
    dot_general x1, matrix products, attend(): jnp.einsum('bhqk,bkhd->bqhd', weights, value_heads, preferred_element_typ...  4.59 us
    all_to_all x1, local copies, waits for them, and re-layouts, sent_to_all(): return lax.all_to_all(copies, axis, split_axis=0, concat_axis=0, tiled=True)  4.15 us
  transfers between devices with their start and end apart: 7, of which 5 were waited for; matrix products, arithmetic and copies ran while one was open for 20% of the time, Pallas kernels for 0%

commit v1 on v0

v1 whole, which is shorter than its diff:
```python
import functools
import math

import jax
import jax.numpy as jnp
from jax import lax
from jax.experimental import pallas as pl
from jax.experimental.pallas import tpu as pltpu
from jax.sharding import PartitionSpec as P

MESH = pl.DeviceIdType.MESH
F32, BF16 = jnp.float32, jnp.bfloat16
DH = 128
RING = 8
SEG = 512
FEAT = 512
CX = 8
RX = SEG // CX
CC = 8
RC = SEG // CC
SCALE = math.log2(math.e) / math.sqrt(DH)
NT = (((1,), (1,)), ((), ()))


def dot(a, b):
    return jnp.dot(a, b, preferred_element_type=F32)


def kernel(n_seg, x_hbm, w_hbm, cw_ref, o_hbm, xb, wb, kv, wide, comp, nb, qb, cb,
           lsem, xs, xr, ks, kr, cs, cr):
    seg, lo = lax.axis_index("seg"), lax.axis_index("head")
    core, hi, block = seg % 2, (seg // 2) % 2, seg // 4
    y = hi * 4 + lo
    n_block = n_seg // 4

    def on_ring(pos):
        return (block * 4 + (pos // 4) * 2 + core, pos % 4)

    up, down = on_ring((y + 1) % RING), on_ring((y + RING - 1) % RING)
    sibling = (block * 4 + hi * 2 + 1 - core, lo)
    after, before = (block + 1) % n_block, (block + n_block - 1) % n_block
    after_same = (after * 4 + hi * 2 + core, lo)
    after_cross = (after * 4 + hi * 2 + 1 - core, lo)
    before_same = (before * 4 + hi * 2 + core, lo)
    before_cross = (before * 4 + hi * 2 + 1 - core, lo)

    own = pltpu.make_async_copy(x_hbm, xb.at[y], lsem.at[0])
    own.start()
    columns = pl.ds(pl.multiple_of(hi * DH, DH), DH)
    loads = []
    for i in range(3):
        load = pltpu.make_async_copy(
            w_hbm.at[i, :, columns], wb.at[:, pl.ds(i * DH, DH)], lsem.at[1 + i]
        )
        load.start()
        loads.append(load)

    barrier = pltpu.get_barrier_semaphore()
    others = (up, down, sibling, after_same, after_cross, before_same, before_cross)
    for other in others:
        pl.semaphore_signal(barrier, inc=1, device_id=other, device_id_type=MESH)
    pl.semaphore_wait(barrier, len(others))
    own.wait()

    def ring_copy(view, ssem, rsem, way, dist, chunk, hop):
        step = dist - hop
        slot = (y + RING - step) % RING if way == 0 else (y + step) % RING
        ref = view(slot, way, dist, chunk, hop)
        return pltpu.make_async_remote_copy(
            src_ref=ref,
            dst_ref=ref,
            send_sem=ssem.at[way, dist - 1, chunk],
            recv_sem=rsem.at[way, dist - 1, chunk],
            device_id=up if way == 0 else down,
            device_id_type=MESH,
        )

    def x_view(slot, way, dist, chunk, hop):
        if dist < 4:
            return xb.at[slot, pl.ds(pl.multiple_of(chunk * RX, RX), RX)]
        half = RX // 2
        return xb.at[slot, pl.ds(pl.multiple_of(chunk * RX + way * half, half), half)]

    def c_view(slot, way, dist, chunk, hop):
        if dist < 4:
            return cb.at[slot, :, pl.ds(pl.multiple_of(chunk * RC, RC), RC)]
        half = RC // 2
        unit = 1 - slot // 4
        return cb.at[slot, unit, pl.ds(pl.multiple_of(chunk * RC + way * half, half), half)]

    x_copy = functools.partial(ring_copy, x_view, xs, xr)
    c_copy = functools.partial(ring_copy, c_view, cs, cr)

    def forward(copy, i, count):
        for dist in (1, 2, 3):
            @pl.when((i >= dist) & (i < count + dist))
            def _(dist=dist):
                for way in (0, 1):
                    copy(way, dist, i - dist, 0).wait_recv()
                    copy(way, dist + 1, i - dist, 1).start()

    def landed(copy, i, count):
        for way in (0, 1):
            copy(way, 4, i - 4, 0).wait_recv()

    def kv_copies(chunk):
        rows = pl.ds(pl.multiple_of(chunk * RX, RX), RX)
        first_core = core == 0
        plan = (
            (4, jnp.where(first_core, 3, 5), sibling),
            (jnp.where(first_core, 6, 4), jnp.where(first_core, 5, 1),
             (jnp.where(first_core, sibling[0], after_cross[0]), lo)),
            (4, 0, after_same),
            (6, 2, after_same),
            (6, jnp.where(first_core, 1, 3), after_cross),
        )
        return [
            pltpu.make_async_remote_copy(
                src_ref=kv.at[src, rows],
                dst_ref=kv.at[dst, rows],
                send_sem=ks.at[n, chunk],
                recv_sem=kr.at[dst, chunk],
                device_id=device,
                device_id_type=MESH,
            )
            for n, (src, dst, device) in enumerate(plan)
        ]

    def project(chunk):
        rows = pl.ds(pl.multiple_of(chunk * RX, RX), RX)
        for u in range(2):
            parts = [xb[4 * u + f, rows, :].astype(F32) for f in range(4)]
            total = parts[0] + parts[1] + parts[2] + parts[3]
            mean = jnp.sum(total, axis=-1, keepdims=True) / (4 * FEAT)
            parts = [p - mean for p in parts]
            square = sum(p * p for p in parts[1:]) + parts[0] * parts[0]
            var = jnp.sum(square, axis=-1, keepdims=True) / (4 * FEAT)
            rstd = lax.rsqrt(var + 1e-05)
            for f in range(4):
                nb[u * RX:(u + 1) * RX, f * FEAT:(f + 1) * FEAT] = (parts[f] * rstd).astype(BF16)
        out = dot(nb[...], wb[...]).astype(BF16)
        for u in range(2):
            part = out[u * RX:(u + 1) * RX]
            qb[u, rows, :] = part[:, :DH]
            kv[4 + 2 * u, rows, :] = part[:, DH:]
        for copy in kv_copies(chunk):
            copy.start()

    for load in loads:
        load.wait()

    def gather(i, _):
        @pl.when(i < CX)
        def _():
            for way in (0, 1):
                x_copy(way, 1, i, 1).start()

        forward(x_copy, i, CX)

        @pl.when(i >= 4)
        def _():
            landed(x_copy, i, CX)
            project(i - 4)
        return 0

    lax.fori_loop(0, CX + 4, gather, 0)

    def kv_wait(chunk, _):
        rows = pl.ds(pl.multiple_of(chunk * RX, RX), RX)
        for dst in (0, 1, 2, 3, 5):
            pltpu.make_async_remote_copy(
                src_ref=kv.at[dst, rows], dst_ref=kv.at[dst, rows], send_sem=ks.at[0, chunk],
                recv_sem=kr.at[dst, chunk], device_id=sibling, device_id_type=MESH,
            ).wait_recv()
        return 0

    lax.fori_loop(0, CX, kv_wait, 0)

    def widen(n, _):
        rows = pl.ds(pl.multiple_of(n * SEG, SEG), SEG)
        wide[0, rows, :] = kv[n][:, :DH].astype(F32)
        wide[1, rows, :] = kv[n][:, DH:].astype(F32)
        return 0

    lax.fori_loop(0, 5, widen, 0)
    taps = cw_ref[:, :, columns].astype(F32)
    for u in range(2):
        for k in range(2):
            mixed = taps[0, k][None, :] * wide[k, pl.ds(1024 * u, SEG, 3), :]
            for r in (1, 2):
                mixed += taps[r, k][None, :] * wide[k, pl.ds(1024 * u + r, SEG, 3), :]
            comp[u, k] = mixed.astype(BF16)

    def attend(u, chunk):
        start = pl.multiple_of(chunk * RC, RC)
        rows = pl.ds(start, RC)
        q = qb[u, rows, :]
        gap = jnp.float32(-1e30)
        no_comp = jnp.where(block >= 1, jnp.float32(0), gap)
        no_mem = jnp.where(block * 4 + core + 2 * u >= 1, jnp.float32(0), gap)
        s_comp = lax.dot_general(q, comp[u, 0], NT, preferred_element_type=F32) + no_comp
        s_mem = lax.dot_general(q, kv[3 + 2 * u, :, :DH], NT, preferred_element_type=F32) + no_mem
        s_own = lax.dot_general(q, kv[4 + 2 * u, :, :DH], NT, preferred_element_type=F32)
        q_pos = start + lax.broadcasted_iota(jnp.int32, (RC, SEG), 0)
        k_pos = lax.broadcasted_iota(jnp.int32, (RC, SEG), 1)
        s_own = jnp.where(k_pos <= q_pos, s_own, gap)
        top = jnp.max(jnp.maximum(jnp.maximum(s_comp, s_mem), s_own), axis=-1, keepdims=True)
        e_comp = jnp.exp2((s_comp - top) * SCALE)
        e_mem = jnp.exp2((s_mem - top) * SCALE)
        e_own = jnp.exp2((s_own - top) * SCALE)
        norm = jnp.sum(e_comp + e_mem + e_own, axis=-1, keepdims=True)
        mixed = dot(e_comp.astype(BF16), comp[u, 1])
        mixed += dot(e_mem.astype(BF16), kv[3 + 2 * u, :, DH:])
        mixed += dot(e_own.astype(BF16), kv[4 + 2 * u, :, DH:])
        cb[y, u, rows, :] = (mixed / norm).astype(BF16)

    def share(i, _):
        @pl.when(i < CC)
        def _():
            for u in range(2):
                attend(u, i)
            for way in (0, 1):
                c_copy(way, 1, i, 1).start()

        forward(c_copy, i, CC)

        @pl.when(i >= 4)
        def _():
            landed(c_copy, i, CC)
        return 0

    lax.fori_loop(0, CC + 4, share, 0)

    stores = []
    for slot in range(RING):
        head = 2 * (slot % 4) + slot // 4
        store = pltpu.make_async_copy(
            cb.at[slot, hi], o_hbm.at[:, pl.ds(head * DH, DH)], lsem.at[4 + slot]
        )
        store.start()
        stores.append(store)

    def sent(chunk, _):
        for way in (0, 1):
            for dist in (1, 2, 3, 4):
                x_copy(way, dist, chunk, 1).wait_send()
                c_copy(way, dist, chunk, 1).wait_send()
        for copy in kv_copies(chunk):
            copy.wait_send()
        return 0

    lax.fori_loop(0, CX, sent, 0)
    for store in stores:
        store.wait()


def local(layer_input, w_qkv, comp_weight, w_out, n_seg):
    whole_out = lax.all_gather(w_out, "seg", axis=0, tiled=True)
    w = jnp.transpose(w_qkv, (1, 0, 2))
    any_spec = pl.BlockSpec(memory_space=pl.ANY)
    vmem_spec = pl.BlockSpec(memory_space=pltpu.VMEM)
    context = pl.pallas_call(
        functools.partial(kernel, n_seg),
        out_shape=jax.ShapeDtypeStruct((SEG, RING * DH), BF16),
        in_specs=[any_spec, any_spec, vmem_spec],
        out_specs=any_spec,
        scratch_shapes=[
            pltpu.VMEM((RING, SEG, FEAT), BF16),
            pltpu.VMEM((4 * FEAT, 3 * DH), BF16),
            pltpu.VMEM((7, SEG, 2 * DH), BF16),
            pltpu.VMEM((2, 5 * SEG + 8, DH), F32),
            pltpu.VMEM((2, 2, SEG, DH), BF16),
            pltpu.VMEM((2 * RX, 4 * FEAT), BF16),
            pltpu.VMEM((2, SEG, DH), BF16),
            pltpu.VMEM((RING, 2, SEG, DH), BF16),
            pltpu.SemaphoreType.DMA((12,)),
            pltpu.SemaphoreType.DMA((2, 4, CX)),
            pltpu.SemaphoreType.DMA((2, 4, CX)),
            pltpu.SemaphoreType.DMA((5, CX)),
            pltpu.SemaphoreType.DMA((7, CX)),
            pltpu.SemaphoreType.DMA((2, 4, CC)),
            pltpu.SemaphoreType.DMA((2, 4, CC)),
        ],
        compiler_params=pltpu.CompilerParams(
            collective_id=0, has_side_effects=True, vmem_limit_bytes=48 << 20
        ),
        cost_estimate=pl.CostEstimate(
            flops=3 * 10**9, bytes_accessed=200 * 10**6, transcendentals=2 * 10**6
        ),
        name="ring_layer",
    )(layer_input[0], w, comp_weight)
    out = jnp.dot(context, whole_out, preferred_element_type=F32)
    return out.astype(BF16)[None]


def solution(mesh):
    return jax.shard_map(
        functools.partial(local, n_seg=mesh.shape["seg"]),
        mesh=mesh,
        in_specs=(
            P(None, "seg", "head"),
            P(None, None, "head"),
            P(None, None, "head"),
            P("seg", "head"),
        ),
        out_specs=P(None, "seg", "head"),
        check_vma=False,
    )
```

time: 190 us -> 142 us (0.75)
  the two profiles are of different devices: /device:TPU:448 before, /device:TPU:1 now
where the time goes in v1:
time: 142 us
  Pallas kernels  98.2 us (69%)
  waiting for transfers between devices  23.6 us (17%)
  between operations  13.4 us (9%)
  local copies, waits for them, and re-layouts  3.61 us (3%)
  matrix products  2.73 us (2%)
    pallas_call x1, Pallas kernels, local(): pl.pallas_call(functools.partial(kernel, n_seg), out_shape=jax.ShapeDtype...  98.2 us
    all_gather x1, waiting for transfers between devices, local(): whole_out = lax.all_gather(w_out, 'seg', axis=0, tiled=True)  22.9 us
    unnamed x6, local copies, waits for them, and re-layouts  3.61 us
  transfers between devices with their start and end apart: 1, of which 1 were waited for; matrix products, arithmetic and copies ran while one was open for 0% of the time, Pallas kernels for 69%

profile of v1, /device:TPU:1, one launch (start us, length us, event | category | flops | bytes accessed | tf_op | source)
XLA Modules:
  0.0 141.6 jit_solution(17679530711009904416)
XLA Ops:
  6.5 0.0 all-gather.2.cloned.1.call-start
  6.5 0.7 all-gather.2.cloned.1.call-update
  7.3 0.0 copy-start
  7.3 1.9 %copy-done = bf16[2048,3,256]{2,0,1:T(8,128)(2,1)S(1)} copy-done((bf16[2048,3,256]{2,0,1:T(8,128)(2,1)S(1)}, bf16[2048,3,256]{2,0,1:T(8,128)(2,1)}, u32[]{:S(2)}) %copy-start) | copy-done | bytes 3145752
  9.1 0.0 copy-start.1
  9.1 1.0 copy-done.1
  10.2 0.0 copy-start.2
  10.2 0.7 copy-done.2
  10.9 98.2 %ring_layer.1 = bf16[512,1024]{1,0:T(8,128)(2,1)S(1)} custom-call(bf16[512,512]{1,0:T(8,128)(2,1)S(1)} %bitcast.7, bf16[3,2048,256]{2,1,0:T(8,128)(2,1)S(1)} %bitcast.6, bf16[3,2,256]{2,1,0:T(2,128)(2,1)S(1)} %copy-done.2), custom_call_target="tpu_custom_call" | custom-call | flops 3000000000 | bytes 200000000 | tf_op jit(solution)/shard_map/ring_layer/pallas_call | solution.py:262
  109.1 22.9 %all-gather.2.cloned.1.call-done = bf16[1024,512]{1,0:T(8,128)(2,1)} async-done(((bf16[8,512]{1,0:T(8,128)(2,1)}), bf16[1024,512]{1,0:T(8,128)(2,1)}) %all-gather.2.cloned.1.call-update) | async-done | bytes 1048592 | tf_op jit(solution)/shard_map/all_gather | solution.py:258
  132.0 2.7 %fusion = bf16[1,512,512]{2,1,0:T(8,128)(2,1)} fusion(bf16[512,1024]{1,0:T(8,128)(2,1)S(1)} %ring_layer.1, bf16[1024,512]{1,0:T(8,128)(2,1)} %all-gather.2.cloned.1.call-done), kind=kOutput, calls=%fused_computation.1 | convolution fusion | flops 537133056 | bytes 2621440 | tf_op jit(solution)/shard_map/dot_general | solution.py:292
Async XLA Ops:
  6.5 125.5 %all-gather.2.cloned.1.call-start = ((), (), s32[]{:S(2)}) async-start(), calls=%async_computation | async-start | bytes 1056768 | tf_op jit(solution)/shard_map/all_gather | solution.py:258
  7.3 1.9 %copy-start = (bf16[2048,3,256]{2,0,1:T(8,128)(2,1)S(1)}, bf16[2048,3,256]{2,0,1:T(8,128)(2,1)}, u32[]{:S(2)}) copy-start(bf16[2048,3,256]{2,0,1:T(8,128)(2,1)} %param.5) | copy-start | bytes 9437188
  9.1 1.0 copy-start.1
  10.2 0.7 copy-start.2
Sparse Core Ops, SparseCore 0:
  12.0 119.9 all-gather.1

commit v2 on v1

--- a/solution.py
+++ b/solution.py
@@ -16,7 +16,9 @@
 FEAT = 512
 CX = 8
 RX = SEG // CX
-CC = 8
+CC = 4
+LAG = 2
+WZ = 5
 RC = SEG // CC
 SCALE = math.log2(math.e) / math.sqrt(DH)
 NT = (((1,), (1,)), ((), ()))
@@ -26,8 +28,8 @@
     return jnp.dot(a, b, preferred_element_type=F32)
 
 
-def kernel(n_seg, x_hbm, w_hbm, cw_ref, o_hbm, xb, wb, kv, wide, comp, nb, qb, cb,
-           lsem, xs, xr, ks, kr, cs, cr):
+def kernel(n_seg, x_hbm, w_hbm, cw_hbm, wo_hbm, o_ref, xb, wb, cw, w8, wo, kv, wide, comp, nb, qb,
+           cb, lsem, xs, xr, ks, kr, cs, cr, ws, wr, kv_ready, z_ready):
     seg, lo = lax.axis_index("seg"), lax.axis_index("head")
     core, hi, block = seg % 2, (seg // 2) % 2, seg // 4
     y = hi * 4 + lo
@@ -44,8 +46,18 @@
     before_same = (before * 4 + hi * 2 + core, lo)
     before_cross = (before * 4 + hi * 2 + 1 - core, lo)
 
+    zed, ex = block // 4, block % 4
+    n_zed = n_block // 4
+    across = (block * 4 + (1 - hi) * 2 + core, lo)
+    rows_x = [((zed * 4 + (ex + d) % 4) * 4 + hi * 2 + core, lo) for d in range(1, 4)]
+    rows_z = [((((zed + d) % n_zed) * 4 + ex) * 4 + hi * 2 + core, lo) for d in range(1, n_zed)]
+
     own = pltpu.make_async_copy(x_hbm, xb.at[y], lsem.at[0])
     own.start()
+    own_out = pltpu.make_async_copy(wo_hbm, w8.at[core], lsem.at[4])
+    own_out.start()
+    taps_in = pltpu.make_async_copy(cw_hbm, cw, lsem.at[5])
+    taps_in.start()
     columns = pl.ds(pl.multiple_of(hi * DH, DH), DH)
     loads = []
     for i in range(3):
@@ -55,12 +67,99 @@
         load.start()
         loads.append(load)
 
+    has_before, has_after = block > 0, block < n_block - 1
+
+    @pl.when(block == 0)
+    def _():
+        kv[0:4] = jnp.zeros((4, SEG, 2 * DH), BF16)
+
     barrier = pltpu.get_barrier_semaphore()
-    others = (up, down, sibling, after_same, after_cross, before_same, before_cross)
-    for other in others:
-        pl.semaphore_signal(barrier, inc=1, device_id=other, device_id_type=MESH)
-    pl.semaphore_wait(barrier, len(others))
+
+    def signal(sem, device):
+        pl.semaphore_signal(sem, inc=1, device_id=device, device_id_type=MESH)
+
+    near = (up, down, sibling, across, *rows_x)
+    for device in near:
+        signal(barrier, device)
+
+    @pl.when(has_after)
+    def _():
+        for device in (after_same, after_cross):
+            signal(barrier, device)
+
+    for d, device in enumerate(rows_z, 1):
+        pl.when(zed + d < n_zed)(functools.partial(signal, barrier, device))
+    pl.semaphore_wait(barrier, len(near) + zed + jnp.where(has_before, 2, 0))
+
+    @pl.when(has_before)
+    def _():
+        for device in (before_same, before_cross):
+            signal(kv_ready, device)
+
+    for d, device in enumerate(rows_z, 1):
+        pl.when(zed + d >= n_zed)(functools.partial(signal, z_ready, device))
     own.wait()
+    own_out.wait()
+
+    def out_copy(n, hop):
+        back = 1 - hop
+        if n == 0:
+            at, device = w8.at[core if hop else 1 - core], sibling
+        elif n == 1:
+            start = (block * 2 + (hi if hop else 1 - hi)) * 16
+            at, device = wo.at[pl.ds(pl.multiple_of(start, 16), 16)], across
+        elif n < 5:
+            d = n - 1
+            start = (zed * 4 + (ex + 4 - d * back) % 4) * 32
+            at, device = wo.at[pl.ds(pl.multiple_of(start, 32), 32)], rows_x[d - 1]
+        else:
+            d = (n - 5) % (n_zed - 1) + 1
+            if n < 4 + n_zed:
+                start = ((zed + n_zed - d * back) % n_zed) * 128 + core * 64
+                device = rows_z[d - 1]
+            else:
+                start = ((zed + n_zed - d) % n_zed) * 128 + (core if hop else 1 - core) * 64
+                device = sibling
+            at = wo.at[pl.ds(pl.multiple_of(start, 64), 64)]
+        return pltpu.make_async_remote_copy(
+            src_ref=at, dst_ref=at, send_sem=ws.at[n], recv_sem=wr.at[n],
+            device_id=device, device_id_type=MESH,
+        )
+
+    out_steps, z_end = 3 + 2 * n_zed, 4 + n_zed
+    out_copy(0, 1).start()
+
+    def gather_out(i):
+        @pl.when(i == 1)
+        def _():
+            out_copy(0, 0).wait_recv()
+            pair = jnp.concatenate([w8[0].astype(F32), w8[1].astype(F32)], axis=0)
+            wo[pl.ds(pl.multiple_of((block * 2 + hi) * 16, 16), 16), :] = pair.astype(BF16)
+            out_copy(1, 1).start()
+
+        @pl.when(i == 2)
+        def _():
+            out_copy(1, 0).wait_recv()
+            for n in range(2, 5):
+                out_copy(n, 1).start()
+
+        @pl.when(i == WZ)
+        def _():
+            for n in range(2, 5):
+                out_copy(n, 0).wait_recv()
+
+            @pl.when(zed < n_zed - 1)
+            def _():
+                pl.semaphore_wait(z_ready, n_zed - 1 - zed)
+
+            for n in range(5, z_end):
+                out_copy(n, 1).start()
+
+        @pl.when(i == CX + 4 * LAG - 3)
+        def _():
+            for n in range(5, z_end):
+                out_copy(n, 0).wait_recv()
+                out_copy(n + n_zed - 1, 1).start()
 
     def ring_copy(view, ssem, rsem, way, dist, chunk, hop):
         step = dist - hop
@@ -93,15 +192,15 @@
 
     def forward(copy, i, count):
         for dist in (1, 2, 3):
-            @pl.when((i >= dist) & (i < count + dist))
+            @pl.when((i >= dist * LAG) & (i < count + dist * LAG))
             def _(dist=dist):
                 for way in (0, 1):
-                    copy(way, dist, i - dist, 0).wait_recv()
-                    copy(way, dist + 1, i - dist, 1).start()
+                    copy(way, dist, i - dist * LAG, 0).wait_recv()
+                    copy(way, dist + 1, i - dist * LAG, 1).start()
 
     def landed(copy, i, count):
         for way in (0, 1):
-            copy(way, 4, i - 4, 0).wait_recv()
+            copy(way, 4, i - 4 * LAG, 0).wait_recv()
 
     def kv_copies(chunk):
         rows = pl.ds(pl.multiple_of(chunk * RX, RX), RX)
@@ -126,6 +225,9 @@
             for n, (src, dst, device) in enumerate(plan)
         ]
 
+    kv_sent = (True, (core == 0) | has_after, has_after, has_after, has_after)
+    kv_received = ((5, True), (3, (core == 1) | has_before), (0, has_before), (1, has_before), (2, has_before))
+
     def project(chunk):
         rows = pl.ds(pl.multiple_of(chunk * RX, RX), RX)
         for u in range(2):
@@ -143,8 +245,8 @@
             part = out[u * RX:(u + 1) * RX]
             qb[u, rows, :] = part[:, :DH]
             kv[4 + 2 * u, rows, :] = part[:, DH:]
-        for copy in kv_copies(chunk):
-            copy.start()
+        for copy, needed in zip(kv_copies(chunk), kv_sent):
+            pl.when(needed)(copy.start)
 
     for load in loads:
         load.wait()
@@ -156,22 +258,29 @@
                 x_copy(way, 1, i, 1).start()
 
         forward(x_copy, i, CX)
-
-        @pl.when(i >= 4)
+        gather_out(i)
+
+        @pl.when(i >= 4 * LAG)
         def _():
             landed(x_copy, i, CX)
-            project(i - 4)
-        return 0
-
-    lax.fori_loop(0, CX + 4, gather, 0)
+
+            @pl.when((i == 4 * LAG) & has_after)
+            def _():
+                pl.semaphore_wait(kv_ready, 2)
+
+            project(i - 4 * LAG)
+        return 0
+
+    lax.fori_loop(0, CX + 4 * LAG, gather, 0)
 
     def kv_wait(chunk, _):
         rows = pl.ds(pl.multiple_of(chunk * RX, RX), RX)
-        for dst in (0, 1, 2, 3, 5):
-            pltpu.make_async_remote_copy(
+        for dst, needed in kv_received:
+            copy = pltpu.make_async_remote_copy(
                 src_ref=kv.at[dst, rows], dst_ref=kv.at[dst, rows], send_sem=ks.at[0, chunk],
                 recv_sem=kr.at[dst, chunk], device_id=sibling, device_id_type=MESH,
-            ).wait_recv()
+            )
+            pl.when(needed)(copy.wait_recv)
         return 0
 
     lax.fori_loop(0, CX, kv_wait, 0)
@@ -183,7 +292,8 @@
         return 0
 
     lax.fori_loop(0, 5, widen, 0)
-    taps = cw_ref[:, :, columns].astype(F32)
+    taps_in.wait()
+    taps = cw[:, :, columns].astype(F32)
     for u in range(2):
         for k in range(2):
             mixed = taps[0, k][None, :] * wide[k, pl.ds(1024 * u, SEG, 3), :]
@@ -224,73 +334,80 @@
 
         forward(c_copy, i, CC)
 
-        @pl.when(i >= 4)
+        @pl.when(i >= 4 * LAG)
         def _():
             landed(c_copy, i, CC)
-        return 0
-
-    lax.fori_loop(0, CC + 4, share, 0)
-
-    stores = []
-    for slot in range(RING):
-        head = 2 * (slot % 4) + slot // 4
-        store = pltpu.make_async_copy(
-            cb.at[slot, hi], o_hbm.at[:, pl.ds(head * DH, DH)], lsem.at[4 + slot]
-        )
-        store.start()
-        stores.append(store)
+            rows = pl.ds(pl.multiple_of((i - 4 * LAG) * RC, RC), RC)
+            whole = jnp.concatenate([cb[slot, hi, rows, :] for slot in (0, 4, 1, 5, 2, 6, 3, 7)], axis=1)
+            o_ref[rows, :] = dot(whole, wo[...]).astype(BF16)
+        return 0
+
+    for n in range(z_end, out_steps):
+        out_copy(n, 0).wait_recv()
+    lax.fori_loop(0, CC + 4 * LAG, share, 0)
 
     def sent(chunk, _):
         for way in (0, 1):
             for dist in (1, 2, 3, 4):
                 x_copy(way, dist, chunk, 1).wait_send()
+        for copy, needed in zip(kv_copies(chunk), kv_sent):
+            pl.when(needed)(copy.wait_send)
+        return 0
+
+    lax.fori_loop(0, CX, sent, 0)
+
+    def c_sent(chunk, _):
+        for way in (0, 1):
+            for dist in (1, 2, 3, 4):
                 c_copy(way, dist, chunk, 1).wait_send()
-        for copy in kv_copies(chunk):
-            copy.wait_send()
-        return 0
-
-    lax.fori_loop(0, CX, sent, 0)
-    for store in stores:
-        store.wait()
+        return 0
+
+    lax.fori_loop(0, CC, c_sent, 0)
+    for n in range(out_steps):
+        out_copy(n, 1).wait_send()
 
 
 def local(layer_input, w_qkv, comp_weight, w_out, n_seg):
-    whole_out = lax.all_gather(w_out, "seg", axis=0, tiled=True)
     w = jnp.transpose(w_qkv, (1, 0, 2))
     any_spec = pl.BlockSpec(memory_space=pl.ANY)
-    vmem_spec = pl.BlockSpec(memory_space=pltpu.VMEM)
-    context = pl.pallas_call(
+    out = pl.pallas_call(
         functools.partial(kernel, n_seg),
-        out_shape=jax.ShapeDtypeStruct((SEG, RING * DH), BF16),
-        in_specs=[any_spec, any_spec, vmem_spec],
-        out_specs=any_spec,
+        out_shape=jax.ShapeDtypeStruct((SEG, FEAT), BF16),
+        in_specs=[any_spec] * 4,
+        out_specs=pl.BlockSpec(memory_space=pltpu.VMEM),
         scratch_shapes=[
             pltpu.VMEM((RING, SEG, FEAT), BF16),
             pltpu.VMEM((4 * FEAT, 3 * DH), BF16),
+            pltpu.VMEM((3, 2, 2 * DH), BF16),
+            pltpu.VMEM((2, 8, FEAT), BF16),
+            pltpu.VMEM((RING * DH, FEAT), BF16),
             pltpu.VMEM((7, SEG, 2 * DH), BF16),
             pltpu.VMEM((2, 5 * SEG + 8, DH), F32),
             pltpu.VMEM((2, 2, SEG, DH), BF16),
             pltpu.VMEM((2 * RX, 4 * FEAT), BF16),
             pltpu.VMEM((2, SEG, DH), BF16),
             pltpu.VMEM((RING, 2, SEG, DH), BF16),
-            pltpu.SemaphoreType.DMA((12,)),
+            pltpu.SemaphoreType.DMA((6,)),
             pltpu.SemaphoreType.DMA((2, 4, CX)),
             pltpu.SemaphoreType.DMA((2, 4, CX)),
             pltpu.SemaphoreType.DMA((5, CX)),
             pltpu.SemaphoreType.DMA((7, CX)),
             pltpu.SemaphoreType.DMA((2, 4, CC)),
             pltpu.SemaphoreType.DMA((2, 4, CC)),
+            pltpu.SemaphoreType.DMA((3 + n_seg // 8,)),
+            pltpu.SemaphoreType.DMA((3 + n_seg // 8,)),
+            pltpu.SemaphoreType.REGULAR,
+            pltpu.SemaphoreType.REGULAR,
         ],
         compiler_params=pltpu.CompilerParams(
-            collective_id=0, has_side_effects=True, vmem_limit_bytes=48 << 20
+            collective_id=0, has_side_effects=True, vmem_limit_bytes=60 << 20
         ),
         cost_estimate=pl.CostEstimate(
             flops=3 * 10**9, bytes_accessed=200 * 10**6, transcendentals=2 * 10**6
         ),
         name="ring_layer",
-    )(layer_input[0], w, comp_weight)
-    out = jnp.dot(context, whole_out, preferred_element_type=F32)
-    return out.astype(BF16)[None]
+    )(layer_input[0], w, comp_weight, w_out)
+    return out[None]
 
 
 def solution(mesh):

time: 142 us -> 89.2 us (0.63)
  the two profiles are of different devices: /device:TPU:1 before, /device:TPU:448 now
where the time goes in v2:
time: 89.2 us; the launch traced here: 89 us
  Pallas kernels  87.1 us (98%)
  local copies, waits for them, and re-layouts  1.87 us (2%)
    pallas_call x1, Pallas kernels, local(): pl.pallas_call(functools.partial(kernel, n_seg), out_shape=jax.ShapeDtype...  87.1 us
    unnamed x1, local copies, waits for them, and re-layouts  1.87 us

profile of v2, /device:TPU:448, one launch (start us, length us, event | category | flops | bytes accessed | tf_op | source)
XLA Modules:
  0.0 89.0 jit_solution(12305976994649576783)
XLA Ops:
  0.0 87.1 %ring_layer.1 = bf16[512,512]{1,0:T(8,128)(2,1)} custom-call(bf16[512,512]{1,0:T(8,128)(2,1)} %bitcast.5, bf16[3,2048,256]{2,1,0:T(8,128)(2,1)} %bitcast.4, bf16[3,2,256]{2,1,0:T(2,128)(2,1)} %cw_hbm.1, bf16[8,512]{1,0:T(8,128)(2,1)} %wo_hbm.1), custom_call_target="tpu_custom_call" | custom-call | flops 3000000000 | bytes 200000000 | tf_op jit(solution)/shard_map/ring_layer/pallas_call | solution.py:373
  87.2 1.9 %copy.6 = bf16[1,512,512]{2,1,0:T(8,128)(2,1)} copy(bf16[1,512,512]{2,1,0:T(8,128)(2,1)} %bitcast.3) | data formatting | bytes 1048576

commit v3 on v2

--- a/solution.py
+++ b/solution.py
@@ -18,10 +18,18 @@
 RX = SEG // CX
 CC = 4
 LAG = 2
-WZ = 5
+LAGC = 3
+WZ = 6
 RC = SEG // CC
 SCALE = math.log2(math.e) / math.sqrt(DH)
 NT = (((1,), (1,)), ((), ()))
+
+
+def when(needed, act):
+    if needed is True:
+        act()
+    else:
+        pl.when(needed)(act)
 
 
 def dot(a, b):
@@ -40,11 +48,8 @@
 
     up, down = on_ring((y + 1) % RING), on_ring((y + RING - 1) % RING)
     sibling = (block * 4 + hi * 2 + 1 - core, lo)
-    after, before = (block + 1) % n_block, (block + n_block - 1) % n_block
-    after_same = (after * 4 + hi * 2 + core, lo)
-    after_cross = (after * 4 + hi * 2 + 1 - core, lo)
-    before_same = (before * 4 + hi * 2 + core, lo)
-    before_cross = (before * 4 + hi * 2 + 1 - core, lo)
+    after = (((block + 1) % n_block) * 4 + hi * 2 + core, lo)
+    before = (((block + n_block - 1) % n_block) * 4 + hi * 2 + core, lo)
 
     zed, ex = block // 4, block % 4
     n_zed = n_block // 4
@@ -82,24 +87,14 @@
     for device in near:
         signal(barrier, device)
 
-    @pl.when(has_after)
-    def _():
-        for device in (after_same, after_cross):
-            signal(barrier, device)
-
+    pl.when(has_after)(functools.partial(signal, barrier, after))
     for d, device in enumerate(rows_z, 1):
         pl.when(zed + d < n_zed)(functools.partial(signal, barrier, device))
-    pl.semaphore_wait(barrier, len(near) + zed + jnp.where(has_before, 2, 0))
-
-    @pl.when(has_before)
-    def _():
-        for device in (before_same, before_cross):
-            signal(kv_ready, device)
-
+    pl.semaphore_wait(barrier, len(near) + zed + jnp.where(has_before, 1, 0))
+
+    pl.when(has_before)(functools.partial(signal, kv_ready, before))
     for d, device in enumerate(rows_z, 1):
         pl.when(zed + d >= n_zed)(functools.partial(signal, z_ready, device))
-    own.wait()
-    own_out.wait()
 
     def out_copy(n, hop):
         back = 1 - hop
@@ -127,9 +122,13 @@
         )
 
     out_steps, z_end = 3 + 2 * n_zed, 4 + n_zed
-    out_copy(0, 1).start()
 
     def gather_out(i):
+        @pl.when(i == 0)
+        def _():
+            own_out.wait()
+            out_copy(0, 1).start()
+
         @pl.when(i == 1)
         def _():
             out_copy(0, 0).wait_recv()
@@ -137,7 +136,7 @@
             wo[pl.ds(pl.multiple_of((block * 2 + hi) * 16, 16), 16), :] = pair.astype(BF16)
             out_copy(1, 1).start()
 
-        @pl.when(i == 2)
+        @pl.when(i == 3)
         def _():
             out_copy(1, 0).wait_recv()
             for n in range(2, 5):
@@ -155,16 +154,11 @@
             for n in range(5, z_end):
                 out_copy(n, 1).start()
 
-        @pl.when(i == CX + 4 * LAG - 3)
-        def _():
-            for n in range(5, z_end):
-                out_copy(n, 0).wait_recv()
-                out_copy(n + n_zed - 1, 1).start()
 
     def ring_copy(view, ssem, rsem, way, dist, chunk, hop):
         step = dist - hop
         slot = (y + RING - step) % RING if way == 0 else (y + step) % RING
-        ref = view(slot, way, dist, chunk, hop)
+        ref = view(slot, way, dist, chunk)
         return pltpu.make_async_remote_copy(
             src_ref=ref,
             dst_ref=ref,
@@ -174,13 +168,13 @@
             device_id_type=MESH,
         )
 
-    def x_view(slot, way, dist, chunk, hop):
+    def x_view(slot, way, dist, chunk):
         if dist < 4:
             return xb.at[slot, pl.ds(pl.multiple_of(chunk * RX, RX), RX)]
         half = RX // 2
         return xb.at[slot, pl.ds(pl.multiple_of(chunk * RX + way * half, half), half)]
 
-    def c_view(slot, way, dist, chunk, hop):
+    def c_view(slot, way, dist, chunk):
         if dist < 4:
             return cb.at[slot, :, pl.ds(pl.multiple_of(chunk * RC, RC), RC)]
         half = RC // 2
@@ -190,28 +184,28 @@
     x_copy = functools.partial(ring_copy, x_view, xs, xr)
     c_copy = functools.partial(ring_copy, c_view, cs, cr)
 
-    def forward(copy, i, count):
+    def forward(copy, i, count, lag=LAG):
         for dist in (1, 2, 3):
-            @pl.when((i >= dist * LAG) & (i < count + dist * LAG))
+            @pl.when((i >= dist * lag) & (i < count + dist * lag))
             def _(dist=dist):
                 for way in (0, 1):
-                    copy(way, dist, i - dist * LAG, 0).wait_recv()
-                    copy(way, dist + 1, i - dist * LAG, 1).start()
-
-    def landed(copy, i, count):
+                    copy(way, dist, i - dist * lag, 0).wait_recv()
+                    copy(way, dist + 1, i - dist * lag, 1).start()
+
+    def landed(copy, i, count, lag=LAG):
         for way in (0, 1):
-            copy(way, 4, i - 4 * LAG, 0).wait_recv()
+            copy(way, 4, i - 4 * lag, 0).wait_recv()
 
     def kv_copies(chunk):
         rows = pl.ds(pl.multiple_of(chunk * RX, RX), RX)
         first_core = core == 0
         plan = (
             (4, jnp.where(first_core, 3, 5), sibling),
-            (jnp.where(first_core, 6, 4), jnp.where(first_core, 5, 1),
-             (jnp.where(first_core, sibling[0], after_cross[0]), lo)),
-            (4, 0, after_same),
-            (6, 2, after_same),
-            (6, jnp.where(first_core, 1, 3), after_cross),
+            (6, 5, sibling),
+            (4, 0, after),
+            (6, 2, after),
+            (jnp.where(first_core, 2, 0), 1, sibling),
+            (2, 3, sibling),
         )
         return [
             pltpu.make_async_remote_copy(
@@ -225,8 +219,22 @@
             for n, (src, dst, device) in enumerate(plan)
         ]
 
-    kv_sent = (True, (core == 0) | has_after, has_after, has_after, has_after)
-    kv_received = ((5, True), (3, (core == 1) | has_before), (0, has_before), (1, has_before), (2, has_before))
+    kv_sent = (True, core == 0, has_after, has_after, has_before, (core == 1) & has_before)
+    kv_received = ((1, has_before), (3, (core == 1) | has_before), (5, True))
+
+    def kv_landed(slots, chunk):
+        rows = pl.ds(pl.multiple_of(chunk * RX, RX), RX)
+        for dst, needed in slots:
+            copy = pltpu.make_async_remote_copy(
+                src_ref=kv.at[dst, rows], dst_ref=kv.at[dst, rows], send_sem=ks.at[0, chunk],
+                recv_sem=kr.at[dst, chunk], device_id=sibling, device_id_type=MESH,
+            )
+            when(needed, copy.wait_recv)
+
+    def relay(chunk):
+        kv_landed(((0, has_before), (2, has_before)), chunk)
+        for copy, needed in zip(kv_copies(chunk)[4:], kv_sent[4:]):
+            when(needed, copy.start)
 
     def project(chunk):
         rows = pl.ds(pl.multiple_of(chunk * RX, RX), RX)
@@ -245,11 +253,10 @@
             part = out[u * RX:(u + 1) * RX]
             qb[u, rows, :] = part[:, :DH]
             kv[4 + 2 * u, rows, :] = part[:, DH:]
-        for copy, needed in zip(kv_copies(chunk), kv_sent):
-            pl.when(needed)(copy.start)
-
-    for load in loads:
-        load.wait()
+        for copy, needed in zip(kv_copies(chunk)[:4], kv_sent[:4]):
+            when(needed, copy.start)
+
+    own.wait()
 
     def gather(i, _):
         @pl.when(i < CX)
@@ -260,27 +267,37 @@
         forward(x_copy, i, CX)
         gather_out(i)
 
+        @pl.when(i == 3)
+        def _():
+            for load in loads:
+                load.wait()
+
         @pl.when(i >= 4 * LAG)
         def _():
             landed(x_copy, i, CX)
 
             @pl.when((i == 4 * LAG) & has_after)
             def _():
-                pl.semaphore_wait(kv_ready, 2)
+                pl.semaphore_wait(kv_ready, 1)
 
             project(i - 4 * LAG)
+
+            @pl.when(i >= 4 * LAG + 3)
+            def _():
+                relay(i - 4 * LAG - 3)
         return 0
 
     lax.fori_loop(0, CX + 4 * LAG, gather, 0)
 
+    for chunk in range(CX - 3, CX):
+        relay(chunk)
+
+    for n in range(5, z_end):
+        out_copy(n, 0).wait_recv()
+        out_copy(n + n_zed - 1, 1).start()
+
     def kv_wait(chunk, _):
-        rows = pl.ds(pl.multiple_of(chunk * RX, RX), RX)
-        for dst, needed in kv_received:
-            copy = pltpu.make_async_remote_copy(
-                src_ref=kv.at[dst, rows], dst_ref=kv.at[dst, rows], send_sem=ks.at[0, chunk],
-                recv_sem=kr.at[dst, chunk], device_id=sibling, device_id_type=MESH,
-            )
-            pl.when(needed)(copy.wait_recv)
+        kv_landed(kv_received, chunk)
         return 0
 
     lax.fori_loop(0, CX, kv_wait, 0)
@@ -332,26 +349,30 @@
             for way in (0, 1):
                 c_copy(way, 1, i, 1).start()
 
-        forward(c_copy, i, CC)
-
-        @pl.when(i >= 4 * LAG)
-        def _():
-            landed(c_copy, i, CC)
-            rows = pl.ds(pl.multiple_of((i - 4 * LAG) * RC, RC), RC)
+        forward(c_copy, i, CC, LAGC)
+
+        @pl.when(i >= 4 * LAGC)
+        def _():
+            landed(c_copy, i, CC, LAGC)
+
+            @pl.when(i == 4 * LAGC)
+            def _():
+                for n in range(z_end, out_steps):
+                    out_copy(n, 0).wait_recv()
+
+            rows = pl.ds(pl.multiple_of((i - 4 * LAGC) * RC, RC), RC)
             whole = jnp.concatenate([cb[slot, hi, rows, :] for slot in (0, 4, 1, 5, 2, 6, 3, 7)], axis=1)
             o_ref[rows, :] = dot(whole, wo[...]).astype(BF16)
         return 0
 
-    for n in range(z_end, out_steps):
-        out_copy(n, 0).wait_recv()
-    lax.fori_loop(0, CC + 4 * LAG, share, 0)
+    lax.fori_loop(0, CC + 4 * LAGC, share, 0)
 
     def sent(chunk, _):
         for way in (0, 1):
             for dist in (1, 2, 3, 4):
                 x_copy(way, dist, chunk, 1).wait_send()
         for copy, needed in zip(kv_copies(chunk), kv_sent):
-            pl.when(needed)(copy.wait_send)
+            when(needed, copy.wait_send)
         return 0
 
     lax.fori_loop(0, CX, sent, 0)
@@ -390,7 +411,7 @@
             pltpu.SemaphoreType.DMA((6,)),
             pltpu.SemaphoreType.DMA((2, 4, CX)),
             pltpu.SemaphoreType.DMA((2, 4, CX)),
-            pltpu.SemaphoreType.DMA((5, CX)),
+            pltpu.SemaphoreType.DMA((6, CX)),
             pltpu.SemaphoreType.DMA((7, CX)),
             pltpu.SemaphoreType.DMA((2, 4, CC)),
             pltpu.SemaphoreType.DMA((2, 4, CC)),

time: 89.2 us -> 86.9 us (0.974)
  Pallas kernels: 87.1 us -> 84.6 us
    pallas_call x1, Pallas kernels: 87.1 us -> 84.6 us  [local(): pl.pallas_call(functools.partial(kernel, n_seg), out_shape=jax.ShapeDtype...]
where the time goes in v3:
time: 86.9 us; the launch traced here: 86.4 us
  Pallas kernels  84.6 us (97%)
  local copies, waits for them, and re-layouts  1.87 us (2%)
    pallas_call x1, Pallas kernels, local(): pl.pallas_call(functools.partial(kernel, n_seg), out_shape=jax.ShapeDtype...  84.6 us
    unnamed x1, local copies, waits for them, and re-layouts  1.87 us

profile of v3, /device:TPU:448, one launch (start us, length us, event | category | flops | bytes accessed | tf_op | source)
XLA Modules:
  0.0 86.4 jit_solution(17859766430166593988)
XLA Ops:
  0.0 84.6 %ring_layer.1 = bf16[512,512]{1,0:T(8,128)(2,1)} custom-call(bf16[512,512]{1,0:T(8,128)(2,1)} %bitcast.5, bf16[3,2048,256]{2,1,0:T(8,128)(2,1)} %bitcast.4, bf16[3,2,256]{2,1,0:T(2,128)(2,1)} %cw_hbm.1, bf16[8,512]{1,0:T(8,128)(2,1)} %wo_hbm.1), custom_call_target="tpu_custom_call" | custom-call | flops 3000000000 | bytes 200000000 | tf_op jit(solution)/shard_map/ring_layer/pallas_call | solution.py:394
  84.6 1.9 %copy.6 = bf16[1,512,512]{2,1,0:T(8,128)(2,1)} copy(bf16[1,512,512]{2,1,0:T(8,128)(2,1)} %bitcast.3) | data formatting | bytes 1048576

commit v4 on v3

--- a/solution.py
+++ b/solution.py
@@ -37,7 +37,7 @@
 
 
 def kernel(n_seg, x_hbm, w_hbm, cw_hbm, wo_hbm, o_ref, xb, wb, cw, w8, wo, kv, wide, comp, nb, qb,
-           cb, lsem, xs, xr, ks, kr, cs, cr, ws, wr, kv_ready, z_ready):
+           cb, lsem, xs, xr, ks, kr, cs, cr, ws, wr, kv_ready, z_ready, x_ready, y_ready):
     seg, lo = lax.axis_index("seg"), lax.axis_index("head")
     core, hi, block = seg % 2, (seg // 2) % 2, seg // 4
     y = hi * 4 + lo
@@ -83,16 +83,22 @@
     def signal(sem, device):
         pl.semaphore_signal(sem, inc=1, device_id=device, device_id_type=MESH)
 
-    near = (up, down, sibling, across, *rows_x)
+    near = (up, down, sibling)
     for device in near:
         signal(barrier, device)
 
     pl.when(has_after)(functools.partial(signal, barrier, after))
+    pl.when(hi == 0)(functools.partial(signal, barrier, across))
+    for d, device in enumerate(rows_x, 1):
+        pl.when(ex + d < 4)(functools.partial(signal, barrier, device))
     for d, device in enumerate(rows_z, 1):
         pl.when(zed + d < n_zed)(functools.partial(signal, barrier, device))
-    pl.semaphore_wait(barrier, len(near) + zed + jnp.where(has_before, 1, 0))
+    pl.semaphore_wait(barrier, len(near) + zed + ex + hi + jnp.where(has_before, 1, 0))
 
     pl.when(has_before)(functools.partial(signal, kv_ready, before))
+    pl.when(hi == 1)(functools.partial(signal, y_ready, across))
+    for d, device in enumerate(rows_x, 1):
+        pl.when(ex + d >= 4)(functools.partial(signal, x_ready, device))
     for d, device in enumerate(rows_z, 1):
         pl.when(zed + d >= n_zed)(functools.partial(signal, z_ready, device))
 
@@ -129,16 +135,26 @@
             own_out.wait()
             out_copy(0, 1).start()
 
-        @pl.when(i == 1)
+        @pl.when(i == 2)
         def _():
             out_copy(0, 0).wait_recv()
             pair = jnp.concatenate([w8[0].astype(F32), w8[1].astype(F32)], axis=0)
             wo[pl.ds(pl.multiple_of((block * 2 + hi) * 16, 16), 16), :] = pair.astype(BF16)
+
+            @pl.when(hi == 0)
+            def _():
+                pl.semaphore_wait(y_ready, 1)
+
             out_copy(1, 1).start()
 
-        @pl.when(i == 3)
+        @pl.when(i == 4)
         def _():
             out_copy(1, 0).wait_recv()
+
+            @pl.when(ex < 3)
+            def _():
+                pl.semaphore_wait(x_ready, 3 - ex)
+
             for n in range(2, 5):
                 out_copy(n, 1).start()
 
@@ -419,6 +435,8 @@
             pltpu.SemaphoreType.DMA((3 + n_seg // 8,)),
             pltpu.SemaphoreType.REGULAR,
             pltpu.SemaphoreType.REGULAR,
+            pltpu.SemaphoreType.REGULAR,
+            pltpu.SemaphoreType.REGULAR,
         ],
         compiler_params=pltpu.CompilerParams(
             collective_id=0, has_side_effects=True, vmem_limit_bytes=60 << 20

time: 86.9 us -> 86 us (0.990)
  Pallas kernels: 84.6 us -> 82.9 us
    pallas_call x1, Pallas kernels: 84.6 us -> 82.9 us  [local(): pl.pallas_call(functools.partial(kernel, n_seg), out_shape=jax.ShapeDtype...]
where the time goes in v4:
time: 86 us; the launch traced here: 84.8 us
  Pallas kernels  82.9 us (96%)
  local copies, waits for them, and re-layouts  1.87 us (2%)
    pallas_call x1, Pallas kernels, local(): pl.pallas_call(functools.partial(kernel, n_seg), out_shape=jax.ShapeDtype...  82.9 us
    unnamed x1, local copies, waits for them, and re-layouts  1.87 us

profile of v4, /device:TPU:448, one launch (start us, length us, event | category | flops | bytes accessed | tf_op | source)
XLA Modules:
  0.0 84.8 jit_solution(16409073321480917498)
XLA Ops:
  0.0 82.9 %ring_layer.1 = bf16[512,512]{1,0:T(8,128)(2,1)} custom-call(bf16[512,512]{1,0:T(8,128)(2,1)} %bitcast.5, bf16[3,2048,256]{2,1,0:T(8,128)(2,1)} %bitcast.4, bf16[3,2,256]{2,1,0:T(2,128)(2,1)} %cw_hbm.1, bf16[8,512]{1,0:T(8,128)(2,1)} %wo_hbm.1), custom_call_target="tpu_custom_call" | custom-call | flops 3000000000 | bytes 200000000 | tf_op jit(solution)/shard_map/ring_layer/pallas_call | solution.py:410
  83.0 1.9 %copy.6 = bf16[1,512,512]{2,1,0:T(8,128)(2,1)} copy(bf16[1,512,512]{2,1,0:T(8,128)(2,1)} %bitcast.3) | data formatting | bytes 1048576

commit v5 on v4

--- a/solution.py
+++ b/solution.py
@@ -190,27 +190,65 @@
         half = RX // 2
         return xb.at[slot, pl.ds(pl.multiple_of(chunk * RX + way * half, half), half)]
 
-    def c_view(slot, way, dist, chunk):
-        if dist < 4:
-            return cb.at[slot, :, pl.ds(pl.multiple_of(chunk * RC, RC), RC)]
-        half = RC // 2
-        unit = 1 - slot // 4
-        return cb.at[slot, unit, pl.ds(pl.multiple_of(chunk * RC + way * half, half), half)]
+    def c_copies(way, dist, chunk, hop):
+        step = dist - hop
+        slot = (y + RING - step) % RING if way == 0 else (y + step) % RING
+        place = slot % 4 if way == 0 else 3 - slot % 4
+        theirs, size = 1 - slot // 4, RC
+        start = pl.multiple_of(chunk * RC, RC)
+
+        def copy(ref):
+            return pltpu.make_async_remote_copy(
+                src_ref=ref, dst_ref=ref, send_sem=cs.at[way, dist - 1, chunk],
+                recv_sem=cr.at[way, dist - 1, chunk],
+                device_id=up if way == 0 else down, device_id_type=MESH,
+            )
+
+        if dist == 4:
+            half = pl.ds(pl.multiple_of(start + way * (size // 2), size // 2), size // 2)
+            return (
+                (place == 3, copy(cb.at[slot, theirs, pl.ds(start, size)])),
+                ((place == 1) | (place == 2), copy(cb.at[slot, theirs, half])),
+            )
+        crossing = place + dist >= 4
+        unit = jnp.where(crossing, theirs, 1 - theirs)
+        single = crossing | (place == 0)
+        return (
+            (single, copy(cb.at[slot, unit, pl.ds(start, size)])),
+            (jnp.logical_not(single), copy(cb.at[slot, :, pl.ds(start, size)])),
+        )
+
+    def c_start(way, dist, chunk):
+        for needed, copy in c_copies(way, dist, chunk, 1):
+            pl.when(needed)(copy.start)
+
+    def c_recv(way, dist, chunk):
+        for needed, copy in c_copies(way, dist, chunk, 0):
+            pl.when(needed)(copy.wait_recv)
+
+    def c_send_done(way, dist, chunk):
+        for needed, copy in c_copies(way, dist, chunk, 1):
+            pl.when(needed)(copy.wait_send)
 
     x_copy = functools.partial(ring_copy, x_view, xs, xr)
-    c_copy = functools.partial(ring_copy, c_view, cs, cr)
-
-    def forward(copy, i, count, lag=LAG):
+
+    def x_start(way, dist, chunk):
+        x_copy(way, dist, chunk, 1).start()
+
+    def x_recv(way, dist, chunk):
+        x_copy(way, dist, chunk, 0).wait_recv()
+
+    def forward(recv, start, i, count, lag=LAG):
         for dist in (1, 2, 3):
             @pl.when((i >= dist * lag) & (i < count + dist * lag))
             def _(dist=dist):
                 for way in (0, 1):
-                    copy(way, dist, i - dist * lag, 0).wait_recv()
-                    copy(way, dist + 1, i - dist * lag, 1).start()
-
-    def landed(copy, i, count, lag=LAG):
+                    recv(way, dist, i - dist * lag)
+                    start(way, dist + 1, i - dist * lag)
+
+    def landed(recv, i, count, lag=LAG):
         for way in (0, 1):
-            copy(way, 4, i - 4 * lag, 0).wait_recv()
+            recv(way, 4, i - 4 * lag)
 
     def kv_copies(chunk):
         rows = pl.ds(pl.multiple_of(chunk * RX, RX), RX)
@@ -280,7 +318,7 @@
             for way in (0, 1):
                 x_copy(way, 1, i, 1).start()
 
-        forward(x_copy, i, CX)
+        forward(x_recv, x_start, i, CX)
         gather_out(i)
 
         @pl.when(i == 3)
@@ -290,7 +328,7 @@
 
         @pl.when(i >= 4 * LAG)
         def _():
-            landed(x_copy, i, CX)
+            landed(x_recv, i, CX)
 
             @pl.when((i == 4 * LAG) & has_after)
             def _():
@@ -363,13 +401,13 @@
             for u in range(2):
                 attend(u, i)
             for way in (0, 1):
-                c_copy(way, 1, i, 1).start()
-
-        forward(c_copy, i, CC, LAGC)
+                c_start(way, 1, i)
+
+        forward(c_recv, c_start, i, CC, LAGC)
 
         @pl.when(i >= 4 * LAGC)
         def _():
-            landed(c_copy, i, CC, LAGC)
+            landed(c_recv, i, CC, LAGC)
 
             @pl.when(i == 4 * LAGC)
             def _():
@@ -396,7 +434,7 @@
     def c_sent(chunk, _):
         for way in (0, 1):
             for dist in (1, 2, 3, 4):
-                c_copy(way, dist, chunk, 1).wait_send()
+                c_send_done(way, dist, chunk)
         return 0
 
     lax.fori_loop(0, CC, c_sent, 0)

time: 86 us -> 83.1 us (0.966)
  Pallas kernels: 82.9 us -> 80.4 us
    pallas_call x1, Pallas kernels: 82.9 us -> 80.4 us  [local(): pl.pallas_call(functools.partial(kernel, n_seg), out_shape=jax.ShapeDtype...]
where the time goes in v5:
time: 83.1 us; the launch traced here: 82.3 us
  Pallas kernels  80.4 us (97%)
  local copies, waits for them, and re-layouts  1.87 us (2%)
    pallas_call x1, Pallas kernels, local(): pl.pallas_call(functools.partial(kernel, n_seg), out_shape=jax.ShapeDtype...  80.4 us
    unnamed x1, local copies, waits for them, and re-layouts  1.87 us

profile of v5, /device:TPU:448, one launch (start us, length us, event | category | flops | bytes accessed | tf_op | source)
XLA Modules:
  0.0 82.3 jit_solution(14490069872072121196)
XLA Ops:
  0.0 80.4 %ring_layer.1 = bf16[512,512]{1,0:T(8,128)(2,1)} custom-call(bf16[512,512]{1,0:T(8,128)(2,1)} %bitcast.5, bf16[3,2048,256]{2,1,0:T(8,128)(2,1)} %bitcast.4, bf16[3,2,256]{2,1,0:T(2,128)(2,1)} %cw_hbm.1, bf16[8,512]{1,0:T(8,128)(2,1)} %wo_hbm.1), custom_call_target="tpu_custom_call" | custom-call | flops 3000000000 | bytes 200000000 | tf_op jit(solution)/shard_map/ring_layer/pallas_call | solution.py:448
  80.4 1.9 %copy.6 = bf16[1,512,512]{2,1,0:T(8,128)(2,1)} copy(bf16[1,512,512]{2,1,0:T(8,128)(2,1)} %bitcast.3) | data formatting | bytes 1048576

commit v6 on v5

--- a/solution.py
+++ b/solution.py
@@ -18,7 +18,7 @@
 RX = SEG // CX
 CC = 4
 LAG = 2
-LAGC = 3
+LAGC = 4
 WZ = 6
 RC = SEG // CC
 SCALE = math.log2(math.e) / math.sqrt(DH)
@@ -285,10 +285,17 @@
             )
             when(needed, copy.wait_recv)
 
+    def widen(n, rows):
+        for k in range(2):
+            to = pl.ds(pl.multiple_of(n * SEG + rows.start, RX), RX)
+            wide[k, to, :] = kv[n, rows, k * DH:(k + 1) * DH].astype(F32)
+
     def relay(chunk):
         kv_landed(((0, has_before), (2, has_before)), chunk)
         for copy, needed in zip(kv_copies(chunk)[4:], kv_sent[4:]):
             when(needed, copy.start)
+        for n in (0, 2, 4):
+            widen(n, pl.ds(pl.multiple_of(chunk * RX, RX), RX))
 
     def project(chunk):
         rows = pl.ds(pl.multiple_of(chunk * RX, RX), RX)
@@ -356,13 +363,12 @@
 
     lax.fori_loop(0, CX, kv_wait, 0)
 
-    def widen(n, _):
-        rows = pl.ds(pl.multiple_of(n * SEG, SEG), SEG)
-        wide[0, rows, :] = kv[n][:, :DH].astype(F32)
-        wide[1, rows, :] = kv[n][:, DH:].astype(F32)
+    def widen_rest(chunk, _):
+        for n in (1, 3):
+            widen(n, pl.ds(pl.multiple_of(chunk * RX, RX), RX))
         return 0
 
-    lax.fori_loop(0, 5, widen, 0)
+    lax.fori_loop(0, CX, widen_rest, 0)
     taps_in.wait()
     taps = cw[:, :, columns].astype(F32)
     for u in range(2):

time: 83.1 us -> 83 us (level)
  no operation moved by 1% of the time
where the time goes in v6:
time: 83 us; the launch traced here: 82.3 us
  Pallas kernels  80.4 us (97%)
  local copies, waits for them, and re-layouts  1.87 us (2%)
    pallas_call x1, Pallas kernels, local(): pl.pallas_call(functools.partial(kernel, n_seg), out_shape=jax.ShapeDtype...  80.4 us
    unnamed x1, local copies, waits for them, and re-layouts  1.87 us

profile of v6, /device:TPU:448, one launch (start us, length us, event | category | flops | bytes accessed | tf_op | source)
XLA Modules:
  0.0 82.3 jit_solution(13704839227695869506)
XLA Ops:
  0.0 80.4 %ring_layer.1 = bf16[512,512]{1,0:T(8,128)(2,1)} custom-call(bf16[512,512]{1,0:T(8,128)(2,1)} %bitcast.5, bf16[3,2048,256]{2,1,0:T(8,128)(2,1)} %bitcast.4, bf16[3,2,256]{2,1,0:T(2,128)(2,1)} %cw_hbm.1, bf16[8,512]{1,0:T(8,128)(2,1)} %wo_hbm.1), custom_call_target="tpu_custom_call" | custom-call | flops 3000000000 | bytes 200000000 | tf_op jit(solution)/shard_map/ring_layer/pallas_call | solution.py:454
  80.4 1.9 %copy.6 = bf16[1,512,512]{2,1,0:T(8,128)(2,1)} copy(bf16[1,512,512]{2,1,0:T(8,128)(2,1)} %bitcast.3) | data formatting | bytes 1048576
